TPU v7x, 256 devices: a whole 4x4x8 slice. The times are simulated.
256 devices in a mesh: dp: 128 (over x_lo, z, y, core), mp: 2 (over x_hi).
Axes of the slice: x: 4 (x_hi: 2, x_lo: 2; x = x_hi * 2 + x_lo), y: 4, z: 8, core: 2. Of those that a mesh axis runs over, the one named last changes fastest.
Arguments:
- image_in: bfloat16 [16384, 1536], P('dp', 'mp'), may hold values from -24 to 24
- text_in: bfloat16 [16384, 1536], P('dp', 'mp'), may hold values from -24 to 24
- image_w: bfloat16 [1536, 1536], P('mp'), may hold values from -0.15625 to 0.15625
- text_w: bfloat16 [1536, 1536], P('mp'), may hold values from -0.15625 to 0.15625
- logit_scale: float32 [], replicated, may hold values from 5 to 15
- logit_bias: float32 [], replicated, may hold values from -5 to -2
Outputs:
- grad_image_in: bfloat16 [16384, 1536], P('dp', 'mp')
- grad_text_in: bfloat16 [16384, 1536], P('dp', 'mp')
- grad_image_w: float32 [1536, 1536], P(('mp', 'dp'))
- grad_text_w: float32 [1536, 1536], P(('mp', 'dp'))
All inputs are finite; a program needn't handle non-finite values.
Results may differ from a plain program's by a relative error of at most 0.0075.
Values may be sent and summed in bfloat16 or wider, within the bound.
A program may use at most 64 MiB of HBM per device.

v0:
```python
import jax
import jax.numpy as jnp
from jax import lax
from jax.sharding import PartitionSpec as P

STEPS = 16


def shifted(block, axis, distance):
    devices = range(lax.axis_size(axis))
    route = [((i - distance) % len(devices), i) for i in devices]
    return lax.ppermute(block, axis, route)


def pair_tile(image_rows, texts, first_row, same_block, scale, bias, total):
    dots = jnp.dot(image_rows, texts.T, preferred_element_type=jnp.float32)
    logits = scale * dots + bias
    rows = first_row + lax.broadcasted_iota(jnp.int32, dots.shape, 0)
    cols = lax.broadcasted_iota(jnp.int32, dots.shape, 1)
    if same_block:
        sign = jnp.where(rows == cols, 1.0, -1.0).astype(jnp.float32)
    else:
        sign = -jnp.ones_like(dots)
    grad = -sign * jax.nn.sigmoid(-sign * logits) / total
    return (scale * grad).astype(jnp.bfloat16)


def text_term(weighted, image_rows):
    return lax.dot_general(
        weighted, image_rows, (((0,), (0,)), ((), ())), preferred_element_type=jnp.float32
    )


def backward(unit, inv_norm, upstream, features, weight):
    dy = (inv_norm * (upstream - unit * jnp.sum(unit * upstream, axis=-1, keepdims=True))).astype(
        jnp.bfloat16
    )
    grad_in = lax.dot_general(
        dy, weight, (((1,), (1,)), ((), ())), preferred_element_type=jnp.float32
    ).astype(jnp.bfloat16)
    grad_w = lax.dot_general(
        features, dy, (((0,), (0,)), ((), ())), preferred_element_type=jnp.float32
    )
    return (grad_in, grad_w)


def local(image_in, text_in, image_w, text_w, logit_scale, logit_bias):
    part_i = jnp.dot(image_in, image_w, preferred_element_type=jnp.float32)
    part_t = jnp.dot(text_in, text_w, preferred_element_type=jnp.float32)
    y_i, y_t = lax.psum((part_i, part_t), "mp")
    norm_i = lax.rsqrt(jnp.sum(y_i * y_i, axis=-1, keepdims=True) + 1e-06)
    norm_t = lax.rsqrt(jnp.sum(y_t * y_t, axis=-1, keepdims=True) + 1e-06)
    unit_i = y_i * norm_i
    unit_t = y_t * norm_t
    emb_i = unit_i.astype(jnp.bfloat16)
    emb_t = unit_t.astype(jnp.bfloat16)
    pairs = emb_i.shape[0]
    half = pairs // lax.axis_size("mp")
    first_row = lax.axis_index("mp") * half
    total = float(pairs * lax.axis_size("dp"))
    my_rows = lax.dynamic_slice_in_dim(emb_i, first_row, half, 0)
    width = emb_i.shape[1]
    weighted = pair_tile(my_rows, emb_t, first_row, True, logit_scale, logit_bias, total)
    d_mine = jnp.dot(weighted, emb_t, preferred_element_type=jnp.float32)
    acc = text_term(weighted, my_rows)

    def carry_step(step, carry):
        texts, sums, d_rows = carry
        texts = shifted(texts, "dp", -1)
        sums = shifted(sums, "dp", -1)
        tile = pair_tile(my_rows, texts, first_row, False, logit_scale, logit_bias, total)
        d_rows = d_rows + jnp.dot(tile, texts, preferred_element_type=jnp.float32)
        sums = sums + text_term(tile, my_rows)
        return (texts, sums, d_rows)

    texts, acc, d_mine = lax.fori_loop(1, STEPS, carry_step, (emb_t, acc, d_mine))
    d_text = shifted(acc, "dp", STEPS - 1)
    d_full = lax.dynamic_update_slice_in_dim(
        jnp.zeros((pairs, width), jnp.float32), d_mine, first_row, 0
    )
    d_image, d_text = lax.psum((d_full, d_text), "mp")
    gx_i, gw_i = backward(unit_i, norm_i, d_image, image_in, image_w)
    gx_t, gw_t = backward(unit_t, norm_t, d_text, text_in, text_w)
    gw_i, gw_t = (
        lax.psum_scatter(gw_i, "dp", scatter_dimension=0, tiled=True),
        lax.psum_scatter(gw_t, "dp", scatter_dimension=0, tiled=True),
    )
    return (gx_i, gx_t, gw_i, gw_t)


def solution(mesh):
    placed = (P("dp", "mp"), P("dp", "mp"), P("mp", None), P("mp", None), P(), P())
    return jax.shard_map(
        local,
        mesh=mesh,
        in_specs=placed,
        out_specs=(P("dp", "mp"), P("dp", "mp"), P(("mp", "dp"), None), P(("mp", "dp"), None)),
        check_vma=False,
    )
```

profile of v0, /device:TPU:1, one launch (start us, length us, event | category | flops | bytes accessed | tf_op | source)
XLA Modules:
  0.0 1638.3 jit_solution(10327951320938826036)
XLA Ops:
  13.3 67.5 %all-reduce.13.cloned.1.call-done = (f32[128,1536]{1,0:T(8,128)}, f32[128,1536]{1,0:T(8,128)}) async-done(((f32[128,1536]{1,0:T(8,128)}, f32[128,1536]{1,0:T(8,128)}), (f32[128,1536]{1,0:T(8,128)}, f32[128,1536]{1,0:T(8,128)})) %all-reduce.13.cloned.1.call-update) | async-done | bytes 1572880 | tf_op jit(solution)/shard_map/psum | solution.py:50
  85.5 328.2 %while.15 = (s32[]{:T(128)}, bf16[128,1536]{1,0:T(8,128)(2,1)}, f32[128,1536]{1,0:T(8,128)}, f32[64,1536]{1,0:T(8,128)S(1)}, f32[]{:T(128)}, /*index=5*/bf16[64,...) while((s32[]{:T(128)}, bf16[128,1536]{1,0:T(8,128)(2,1)}, f32[128,1536]{1,0:T(8,128)}, ...), condition=%wide.region_5.6_spmd, body=%wide.region_4.5_spmd.sunk | while | flops 75849728 | bytes 9093305 | solution.py:76
  107.5 6.1 collective-permute-start.1
  122.1 7.9 collective-permute-start
  130.0 6.1 collective-permute-start.1
  144.1 8.4 collective-permute-start
  152.5 6.1 collective-permute-start.1
  166.5 8.4 collective-permute-start
  175.0 6.1 collective-permute-start.1
  189.0 8.4 collective-permute-start
  197.4 6.1 collective-permute-start.1
  211.5 8.4 collective-permute-start
  219.9 6.1 collective-permute-start.1
  233.9 8.4 collective-permute-start
  256.4 8.4 collective-permute-start
  278.9 8.4 collective-permute-start
  301.3 8.4 collective-permute-start
  323.8 8.4 collective-permute-start
  346.3 8.4 collective-permute-start
  368.7 8.4 collective-permute-start
  391.2 8.4 collective-permute-start
  414.7 21.1 %collective-permute-done.2 = f32[128,1536]{1,0:T(8,128)} collective-permute-done((f32[128,1536]{1,0:T(8,128)}, f32[128,1536]{1,0:T(8,128)}, u32[]{:S(2)}, u32[]{:S(2)}) %collective-permute-start.2) | collective-permute-done | bytes 786464 | tf_op jit(solution)/shard_map/ppermute | solution.py:12
  435.9 67.2 %all-reduce.11.cloned.1.call-done = (f32[128,1536]{1,0:T(8,128)}, f32[128,1536]{1,0:T(8,128)}) async-done(((f32[128,1536]{1,0:T(8,128)}, f32[128,1536]{1,0:T(8,128)}), (f32[128,1536]{1,0:T(8,128)}, f32[128,1536]{1,0:T(8,128)})) %all-reduce.11.cloned.1.call-update) | async-done | bytes 1572880 | tf_op jit(solution)/shard_map/psum | solution.py:81
  517.5 1109.2 %all-reduce.9.cloned.1.call-done = (f32[768,1536]{0,1:T(8,128)}, f32[768,1536]{0,1:T(8,128)}) async-done(((f32[768,1536]{0,1:T(8,128)}, f32[768,1536]{0,1:T(8,128)}), (f32[768,1536]{0,1:T(8,128)}, f32[768,1536]{0,1:T(8,128)})) %all-reduce.9.cloned.1.call-update) | async-done | bytes 9437200
  (159 shorter events, 211.3 us)
Async XLA Ops:
  7.2 73.6 %all-reduce.13.cloned.1.call-start = ((), (), s32[]{:S(2)}) async-start(), calls=%async_computation.2 | async-start | bytes 3145728 | tf_op jit(solution)/shard_map/psum | solution.py:50
  11.9 491.2 %all-reduce.11.cloned.1.call-start = ((), (), s32[]{:S(2)}) async-start(), calls=%async_computation.1 | async-start | bytes 3145728 | tf_op jit(solution)/shard_map/psum | solution.py:81
  86.3 15.3 collective-permute-start.1
  107.5 12.3 collective-permute-start.1
  122.1 14.0 collective-permute-start
  144.1 14.6 collective-permute-start
  166.5 14.6 collective-permute-start
  175.0 11.7 collective-permute-start.1
  189.0 14.6 collective-permute-start
  197.4 11.7 collective-permute-start.1
  211.5 14.6 collective-permute-start
  233.9 14.6 collective-permute-start
  242.4 11.7 collective-permute-start.1
  256.4 14.6 collective-permute-start
  278.9 14.6 collective-permute-start
  287.3 11.7 collective-permute-start.1
  301.3 14.6 collective-permute-start
  323.8 14.6 collective-permute-start
  332.2 11.7 collective-permute-start.1
  346.3 14.6 collective-permute-start
  368.7 14.6 collective-permute-start
  391.2 14.6 collective-permute-start
  413.7 22.1 %collective-permute-start.2 = (f32[128,1536]{1,0:T(8,128)}, f32[128,1536]{1,0:T(8,128)}, u32[]{:S(2)}, u32[]{:S(2)}) collective-permute-start(f32[128,1536]{1,0:T(8,128)} %get-tuple-element.76), channel_id=1, source_target_pairs={{226,0},{228,2},{230,4},{232,6},{234,8},{236,10},{238,12},{240,14}... | collective-permute-start | bytes 2359304 | tf_op jit(solution)/shard_map/ppermute | solution.py:12
  435.8 1190.8 %all-reduce.9.cloned.1.call-start = ((), (), s32[]{:S(2)}) async-start(), calls=%async_computation | async-start | bytes 18874368
  (22 other events, 225.9 us)
Sparse Core Ops, SparseCore 0:
  12.0 68.6 all-reduce.12
  436.0 67.0 all-reduce.10
  512.5 1114.1 all-reduce.8
where the time goes:
time: 1640 us
  waiting for transfers between devices  1320 us (80%)
  starting transfers between devices  204 us (12%)
  matrix products  76.3 us (5%)
  local copies, waits for them, and re-layouts  18.8 us (1%)
    unnamed x4, waiting for transfers between devices  1110 us
    ppermute x31, starting transfers between devices, shifted(): return lax.ppermute(block, axis, route)  204 us
    ppermute x31, waiting for transfers between devices, shifted(): return lax.ppermute(block, axis, route)  72.7 us
    psum x1, waiting for transfers between devices, local(): y_i, y_t = lax.psum((part_i, part_t), 'mp')  67.5 us
    psum x1, waiting for transfers between devices, local(): d_image, d_text = lax.psum((d_full, d_text), 'mp')  67.2 us
    dot_general x16, matrix products, text_term(): lax.dot_general(weighted, image_rows, (((0,), (0,)), ((), ())), preferred...  35.7 us
  transfers between devices with their start and end apart: 34, of which 20 were waited for; matrix products, arithmetic and copies ran while one was open for 3% of the time, Pallas kernels for 0%

commit v1 on v0

v1 whole, which is shorter than its diff:
```python
import jax
import jax.numpy as jnp
from jax import lax
from jax.experimental import pallas as pl
from jax.experimental.pallas import tpu as pltpu
from jax.sharding import PartitionSpec as P

MESH = pl.DeviceIdType.MESH
F32, BF16 = jnp.float32, jnp.bfloat16
ROWS = 128
HALF = 768
E = 1536
NY, NZ = 4, 8
SLICE = E // NY
STEPS = 16
SLOTS = 9
NCH = 2
CH = ROWS // NCH
PAIRS = 16384.0


def contract(a, b, da, db):
    return lax.dot_general(a, b, (((da,), (db,)), ((), ())), preferred_element_type=F32)


def body(
    image_in, text_in, image_w, text_w, scale_ref, bias_ref,
    gxi_ref, gxt_ref, gwi_ref, gwt_ref,
    x, w, part, px_send, px_recv, buf, own, y_own, inv_own, weights, acc, d_recv,
    dy, dy_slices, dy_other, gx, xg, dyg, g_send, xr, z_send, zr, f_send, f_recv,
    ld_sem, xg_ss, xg_rs, px_ss, px_rs, zs_ss, ys_ss, bf_rs, ow_ss, ow_rs, d_ss, d_rs,
    x2_ss, x2_rs, dg_ss, dg_rs, xr_ss, xr_rs, z_ss, z_rs, f_ss, f_rs,
):
    dp, r = lax.axis_index("dp"), lax.axis_index("mp")
    h, y, z, xl = dp % 2, (dp // 2) % NY, (dp // 8) % NZ, dp // 64
    m = dp + r * (127 - 2 * dp)
    hh, my, plane = m % 2, (m // 2) % NY, m // 8

    def at(xl_, z_, y_, core, mp):
        return (((xl_ * NZ + z_) * NY + y_) * 2 + core, mp)

    def mirrored(m_):
        return (m_ + r * (127 - 2 * m_), r)

    sibling = at(xl, z, y, 1 - h, r)
    partner = at(xl, z, y, h, 1 - r)
    across = at(1 - xl, z, y, r, h)

    pending = []

    def send(src, dst, ss, rs, device, when=None):
        def copy():
            return pltpu.make_async_remote_copy(
                src_ref=src, dst_ref=dst, send_sem=ss, recv_sem=rs, device_id=device, device_id_type=MESH
            )

        if when is None:
            copy().start()
            pending.append(lambda: copy().wait_send())
        else:

            @pl.when(when)
            def _():
                copy().start()

            def finish():
                @pl.when(when)
                def _():
                    copy().wait_send()

            pending.append(finish)

    def arrived(dst, rs):
        pltpu.make_async_copy(dst, dst, rs).wait()

    def load(src, dst, i):
        copy = pltpu.make_async_copy(src, dst, ld_sem.at[i])
        copy.start()
        return copy

    loads = [
        load(image_in, x.at[0], 0),
        load(text_in, x.at[1], 1),
        load(image_w, w.at[0], 2),
        load(text_w, w.at[1], 3),
    ]
    bar = pltpu.get_barrier_semaphore()
    peers = [sibling, partner, at(xl, z, y, 1 - h, 1 - r), across]
    peers += [at(xl, z, (y + d) % NY, c, r) for d in range(1, NY) for c in (0, 1)]
    peers += [at(xl, (z + d) % NZ, y, h, r) for d in range(1, NZ)]
    peers += [mirrored((m + 8) % 128), mirrored((m + 120) % 128)]
    for peer in peers:
        pl.semaphore_signal(bar, inc=1, device_id=peer, device_id_type=MESH)
    for copy in loads[:2]:
        copy.wait()
    pl.semaphore_wait(bar, len(peers))

    mine = 2 * y + h
    send(x.at[1 - r], xg.at[mine], xg_ss.at[0], xg_rs.at[mine], at(xl, z, y, r, 1 - r))
    for d in range(1, NY):
        send(x.at[r], xg.at[mine], xg_ss.at[d], xg_rs.at[mine], at(xl, z, (y + d) % NY, r, r))
    send(x.at[r], xg.at[mine], xg_ss.at[4], xg_rs.at[mine], sibling, hh == 1)

    @pl.when(hh == 0)
    def _():
        pltpu.make_async_copy(x.at[r], xg.at[mine], xg_rs.at[mine]).start()

    for copy in loads[2:]:
        copy.wait()
    for k, tower in ((0, r), (1, 1 - r)):
        features = x[tower]

        def column(i, c, k=k, tower=tower, features=features):
            cols = pl.ds(pl.multiple_of(i * 256, 256), 256)
            p = jnp.dot(features, w[tower, :, cols], preferred_element_type=F32)
            part[k, :, cols] = p
            px_send[k, :, cols] = p.astype(BF16)
            return c

        lax.fori_loop(0, E // 256, column, 0)
        for c in range(NCH):
            rows = pl.ds(c * CH, CH)
            send(px_send.at[k, rows], px_recv.at[k, rows], px_ss.at[k, c], px_rs.at[k, c], partner)

    for c in range(2):
        slot = 2 * y + c

        @pl.when(hh == 1)
        def _():
            arrived(xg.at[slot], xg_rs.at[slot])

        for d in range(1, NY):
            send(
                xg.at[slot], xg.at[slot], xg_ss.at[4 + 3 * c + d], xg_rs.at[slot],
                at(xl, z, (y + d) % NY, h, r), hh == 1,
            )

    def slot_rows(j, c):
        return pl.ds(pl.multiple_of(j * ROWS + c * CH, CH), CH)

    def y_peer(d):
        return mirrored(plane * 8 + ((my + d) % NY) * 2 + hh)

    z_peer = mirrored((m + 120) % 128)

    for c in range(NCH):
        rows = pl.ds(c * CH, CH)
        arrived(px_recv.at[0, rows], px_rs.at[0, c])
        yy = part[1, rows, :] + px_recv[0, rows, :].astype(F32)
        inv = lax.rsqrt(jnp.sum(yy * yy, axis=-1, keepdims=True) + 1e-06)
        buf[slot_rows(0, c), :] = (yy * inv).astype(BF16)
        src = buf.at[slot_rows(0, c)]
        send(src, buf.at[slot_rows(4, c)], zs_ss.at[0, c], bf_rs.at[4, c], z_peer)
        for d in range(1, NY):
            send(
                src, buf.at[slot_rows(4 - d, c)], ys_ss.at[0, d - 1, c], bf_rs.at[4 - d, c],
                y_peer(d), my + d >= NY,
            )
    for c in range(NCH):
        src = buf.at[slot_rows(4, c)]
        arrived(src, bf_rs.at[4, c])
        send(src, buf.at[slot_rows(8, c)], zs_ss.at[1, c], bf_rs.at[8, c], z_peer)
        for d in range(1, NY):
            slot = 4 - d + 4 * ((my + d) // NY)
            send(src, buf.at[slot_rows(slot, c)], ys_ss.at[1, d - 1, c], bf_rs.at[slot, c], y_peer(d))
    for c in range(NCH):
        rows = pl.ds(c * CH, CH)
        arrived(px_recv.at[1, rows], px_rs.at[1, c])
        yy = part[0, rows, :] + px_recv[1, rows, :].astype(F32)
        inv = lax.rsqrt(jnp.sum(yy * yy, axis=-1, keepdims=True) + 1e-06)
        unit = yy * inv
        y_own[rows, :] = unit
        inv_own[rows, :] = inv
        own[hh, rows, :] = unit.astype(BF16)
    send(own.at[hh], own.at[hh], ow_ss, ow_rs, sibling)
    for c in range(NCH):
        src = buf.at[slot_rows(8, c)]
        arrived(src, bf_rs.at[8, c])
        for d in range(1, NY):
            send(
                src, buf.at[slot_rows(8 - d, c)], ys_ss.at[2, d - 1, c], bf_rs.at[8 - d, c],
                y_peer(d), my + d < NY,
            )
    arrived(own.at[1 - hh], ow_rs)

    scale, bias = scale_ref[0, 0], bias_ref[0, 0]
    for j in (0, 4, 8, 3, 2, 1, 7, 6, 5):
        if j not in (0, 4, 8):
            for c in range(NCH):
                arrived(buf.at[slot_rows(j, c)], bf_rs.at[j, c])
        cols = pl.ds(j * ROWS, ROWS)
        for a in range(2):
            dots = contract(own[a], buf[cols, :], 1, 1)
            logits = scale * dots + bias
            if j == 0:
                diagonal = lax.broadcasted_iota(jnp.int32, dots.shape, 0) == lax.broadcasted_iota(
                    jnp.int32, dots.shape, 1
                )
                same = jnp.logical_and(diagonal, hh == a)
                sign = jnp.where(same, 1.0, -1.0)
                grad = -sign * jax.nn.sigmoid(-sign * logits) / PAIRS
            else:
                grad = jax.nn.sigmoid(logits) / PAIRS
            offset = 2 * j + hh - a
            met = jnp.logical_and(offset >= 0, offset < STEPS)
            weights[a, :, cols] = jnp.where(met, scale * grad, 0.0).astype(BF16)

    for k, a in ((0, 1 - hh), (1, hh)):
        weighted = weights[a]

        def column(i, c, k=k, weighted=weighted):
            cols = pl.ds(pl.multiple_of(i * 256, 256), 256)
            acc[k, :, cols] = jnp.dot(weighted, buf[:, cols], preferred_element_type=F32)
            return c

        lax.fori_loop(0, E // 256, column, 0)
        if k == 0:
            send(acc.at[0], d_recv, d_ss, d_rs, sibling)
    arrived(d_recv, d_rs)
    d_own = acc[1] + d_recv[...]
    unit = y_own[...]
    up = (inv_own[...] * (d_own - unit * jnp.sum(unit * d_own, axis=-1, keepdims=True))).astype(BF16)
    dy[...] = up
    for k in range(NY):
        dy_slices[k] = up[:, k * SLICE : (k + 1) * SLICE]
    send(dy, dy_other, x2_ss, x2_rs, partner)
    for d in range(1, NY):
        to = (y + d) % NY
        send(dy_slices.at[to], dyg.at[mine], dg_ss.at[d - 1], dg_rs.at[mine], at(xl, z, to, h, r))
    dyg[mine] = dy_slices[y]
    send(dyg.at[mine], dyg.at[mine], dg_ss.at[3], dg_rs.at[mine], sibling)

    def input_grad(dy_ref, tower):
        def column(i, c):
            cols = pl.ds(pl.multiple_of(i * 256, 256), 256)
            gx[tower, :, cols] = contract(dy_ref[...], w[tower, cols, :], 1, 1).astype(BF16)
            return c

        lax.fori_loop(0, HALF // 256, column, 0)

    input_grad(dy, r)
    for d in range(1, NY):
        slot = 2 * ((y + d) % NY) + h
        arrived(dyg.at[slot], dg_rs.at[slot])
        send(dyg.at[slot], dyg.at[slot], dg_ss.at[3 + d], dg_rs.at[slot], sibling)
    for d in range(NY):
        slot = 2 * ((y + d) % NY) + 1 - h
        arrived(dyg.at[slot], dg_rs.at[slot])

    for slot in range(8):
        @pl.when(jnp.logical_or(hh == 0, slot // 2 != y))
        def _():
            arrived(xg.at[slot], xg_rs.at[slot])

    ups = dyg[...].reshape(8 * ROWS, SLICE)

    def weight_rows(i, c):
        cols = pl.ds(pl.multiple_of(i * 384, 128), 384)
        g = contract(xg[:, :, cols].reshape(8 * ROWS, 384), ups, 0, 0)
        g_send[i] = g.astype(BF16)
        return c

    lax.fori_loop(0, 2, weight_rows, 0)
    send(g_send.at[1 - xl], xr.at[xl], xr_ss.at[0], xr_rs.at[xl], across)
    send(g_send.at[xl], xr.at[xl], xr_ss.at[1], xr_rs.at[xl], at(xl, z, y, r, h), hh == 1)

    @pl.when(hh == 0)
    def _():
        pltpu.make_async_copy(g_send.at[xl], xr.at[xl], xr_rs.at[xl]).start()

    arrived(dy_other, x2_rs)
    input_grad(dy_other, 1 - r)
    gxi_ref[...] = gx[0]
    gxt_ref[...] = gx[1]

    for k in range(2):
        arrived(xr.at[k], xr_rs.at[k])
    z_send[...] = (xr[0].astype(F32) + xr[1].astype(F32)).astype(BF16).reshape(NZ, 48, SLICE)
    for d in range(1, NZ):
        to = (z + d) % NZ
        send(z_send.at[to], zr.at[z], z_ss.at[d - 1], z_rs.at[z], at(xl, to, y, h, r))
    total = z_send[z].astype(F32)
    for d in range(1, NZ):
        slot = (z + d) % NZ
        arrived(zr.at[slot], z_rs.at[slot])
        total = total + zr[slot].astype(F32)
    for k in range(8):
        f_send[k, 0:6, :] = total[6 * k : 6 * k + 6, :]
        f_send[k, 6:8, :] = jnp.zeros((2, SLICE), F32)
    f_recv[h, y] = f_send[mine]
    for d in range(NY):
        to = (y + d) % NY
        for c in range(2):
            if d == 0 and c == 0:
                continue
            core = (h + c) % 2
            send(
                f_send.at[2 * to + core], f_recv.at[h, y], f_ss.at[2 * d + c], f_rs.at[h, y],
                at(xl, z, to, core, r),
            )
    for d in range(NY):
        for c in range(2):
            if d == 0 and c == 0:
                continue
            core, frm = (h + c) % 2, (y + d) % NY
            arrived(f_recv.at[core, frm], f_rs.at[core, frm])
    for k in range(NY):
        cols = pl.ds(k * SLICE, SLICE)
        gwi_ref[:, cols] = f_recv[0, k, 0:6, :]
        gwt_ref[:, cols] = f_recv[1, k, 0:6, :]
    for finish in pending:
        finish()


def local(image_in, text_in, image_w, text_w, logit_scale, logit_bias):
    hbm = pl.BlockSpec(memory_space=pl.ANY)
    vmem = pl.BlockSpec(memory_space=pltpu.VMEM)
    smem = pl.BlockSpec(memory_space=pltpu.SMEM)
    dma = pltpu.SemaphoreType.DMA
    return pl.pallas_call(
        body,
        name="contrast",
        out_shape=(
            jax.ShapeDtypeStruct((ROWS, HALF), BF16),
            jax.ShapeDtypeStruct((ROWS, HALF), BF16),
            jax.ShapeDtypeStruct((6, E), F32),
            jax.ShapeDtypeStruct((6, E), F32),
        ),
        in_specs=[hbm] * 4 + [smem] * 2,
        out_specs=(vmem,) * 4,
        scratch_shapes=[
            pltpu.VMEM((2, ROWS, HALF), BF16),
            pltpu.VMEM((2, HALF, E), BF16),
            pltpu.VMEM((2, ROWS, E), F32),
            pltpu.VMEM((2, ROWS, E), BF16),
            pltpu.VMEM((2, ROWS, E), BF16),
            pltpu.VMEM((SLOTS * ROWS, E), BF16),
            pltpu.VMEM((2, ROWS, E), BF16),
            pltpu.VMEM((ROWS, E), F32),
            pltpu.VMEM((ROWS, 1), F32),
            pltpu.VMEM((2, ROWS, SLOTS * ROWS), BF16),
            pltpu.VMEM((2, ROWS, E), F32),
            pltpu.VMEM((ROWS, E), F32),
            pltpu.VMEM((ROWS, E), BF16),
            pltpu.VMEM((NY, ROWS, SLICE), BF16),
            pltpu.VMEM((ROWS, E), BF16),
            pltpu.VMEM((2, ROWS, HALF), BF16),
            pltpu.VMEM((8, ROWS, HALF), BF16),
            pltpu.VMEM((8, ROWS, SLICE), BF16),
            pltpu.VMEM((2, HALF // 2, SLICE), BF16),
            pltpu.VMEM((2, HALF // 2, SLICE), BF16),
            pltpu.VMEM((NZ, 48, SLICE), BF16),
            pltpu.VMEM((NZ, 48, SLICE), BF16),
            pltpu.VMEM((8, 8, SLICE), F32),
            pltpu.VMEM((2, NY, 8, SLICE), F32),
            dma((4,)),
            dma((11,)),
            dma((8,)),
            dma((2, NCH)),
            dma((2, NCH)),
            dma((2, NCH)),
            dma((3, 3, NCH)),
            dma((SLOTS, NCH)),
            dma, dma,
            dma, dma,
            dma, dma,
            dma((7,)),
            dma((8,)),
            dma((2,)),
            dma((2,)),
            dma((7,)),
            dma((8,)),
            dma((8,)),
            dma((2, NY)),
        ],
        compiler_params=pltpu.CompilerParams(
            collective_id=0, has_side_effects=True, vmem_limit_bytes=48 << 20
        ),
    )(image_in, text_in, image_w, text_w, logit_scale.reshape(1, 1), logit_bias.reshape(1, 1))


def solution(mesh):
    placed = (P("dp", "mp"), P("dp", "mp"), P("mp", None), P("mp", None), P(), P())
    return jax.shard_map(
        local,
        mesh=mesh,
        in_specs=placed,
        out_specs=(P("dp", "mp"), P("dp", "mp"), P(("mp", "dp"), None), P(("mp", "dp"), None)),
        check_vma=False,
    )
```

time: 1640 us -> 110 us (0.07)
  waiting for transfers between devices: 1320 us -> 0 us
  starting transfers between devices: 204 us -> 0 us
  Pallas kernels: 0 us -> 100 us
  matrix products: 76.3 us -> 0 us
    unnamed x4 -> x0, waiting for transfers between devices: 1110 us -> none
    ppermute x31 -> x0, starting transfers between devices: 204 us -> none  [shifted(): return lax.ppermute(block, axis, route)]
    psum x2 -> x0, waiting for transfers between devices: 135 us -> none  [the longest x1 67.5 us: local(): y_i, y_t = lax.psum((part_i, part_t), 'mp')]
    pallas_call x0 -> x1, Pallas kernels: none -> 100 us  [local(): pl.pallas_call(body, name='contrast', out_shape=(jax.ShapeDtypeStruct((RO...]
    dot_general x54 -> x0, matrix products: 76.3 us -> none  [the longest x16 35.7 us: text_term(): lax.dot_general(weighted, image_rows, (((0,), (0,)), ((), ())), preferred...]
    ppermute x31 -> x0, waiting for transfers between devices: 72.7 us -> none  [shifted(): return lax.ppermute(block, axis, route)]
  transfers between devices with their start and end apart: 34 -> 0, of which waited for: 20 -> 0; matrix products, arithmetic and copies ran while one was open for 3% -> 0% of each run, Pallas kernels for 0% -> 0%
where the time goes in v1:
time: 110 us
  Pallas kernels  100 us (91%)
  local copies, waits for them, and re-layouts  7.77 us (7%)
  between operations  1.95 us (2%)
    pallas_call x1, Pallas kernels, local(): pl.pallas_call(body, name='contrast', out_shape=(jax.ShapeDtypeStruct((RO...  100 us
    unnamed x12, local copies, waits for them, and re-layouts  7.77 us

profile of v1, /device:TPU:1, one launch (start us, length us, event | category | flops | bytes accessed | tf_op | source)
XLA Modules:
  0.0 109.9 jit_solution(9517773324632328413)
XLA Ops:
  1.9 0.0 copy-start
  1.9 1.7 %copy-done = bf16[768,1536]{1,0:T(8,128)(2,1)S(1)} copy-done((bf16[768,1536]{1,0:T(8,128)(2,1)S(1)}, bf16[768,1536]{1,0:T(8,128)(2,1)}, u32[]{:S(2)}) %copy-start) | copy-done | bytes 2359320
  3.6 0.0 copy-start.1
  3.6 1.7 %copy-done.1 = bf16[768,1536]{1,0:T(8,128)(2,1)S(1)} copy-done((bf16[768,1536]{1,0:T(8,128)(2,1)S(1)}, bf16[768,1536]{1,0:T(8,128)(2,1)}, u32[]{:S(2)}) %copy-start.1) | copy-done | bytes 2359320
  5.3 0.0 copy-start.2
  5.3 0.9 copy-done.2
  6.2 0.0 copy-start.3
  6.2 0.9 copy-done.3
  7.1 100.2 %contrast.1 = (bf16[128,768]{1,0:T(8,128)(2,1)S(1)}, bf16[128,768]{1,0:T(8,128)(2,1)S(1)}, f32[6,1536]{1,0:T(8,128)S(1)}, f32[6,1536]{1,0:T(8,128)S(1)}) custom-call(bf16[128,768]{1,0:T(8,128)(2,1)S(1)} %copy-done.2, bf16[128,768]{1,0:T(8,128)(2,1)S(1)} %copy-done.3, bf16[768,1536]{1,0:T(8,128)(2,1)S(1)} %copy-done, bf16[768,1536]{1,0:T(8,128)(2,1)S(1)} %copy-done.1, ...), custom_call_target="tpu_custom_call" | custom-call | tf_op jit(solution)/shard_map/contrast/pallas_call | solution.py:320
  107.3 0.7 copy.16
  108.0 0.7 copy.17
  108.7 0.6 copy.18
  109.3 0.6 copy.19
Async XLA Ops:
  1.9 1.7 %copy-start = (bf16[768,1536]{1,0:T(8,128)(2,1)S(1)}, bf16[768,1536]{1,0:T(8,128)(2,1)}, u32[]{:S(2)}) copy-start(bf16[768,1536]{1,0:T(8,128)(2,1)} %image_w.1) | copy-start | bytes 7077892
  3.6 1.7 %copy-start.1 = (bf16[768,1536]{1,0:T(8,128)(2,1)S(1)}, bf16[768,1536]{1,0:T(8,128)(2,1)}, u32[]{:S(2)}) copy-start(bf16[768,1536]{1,0:T(8,128)(2,1)} %text_w.1) | copy-start | bytes 7077892
  5.3 0.9 copy-start.2
  6.2 0.9 copy-start.3

commit v2 on v1

--- a/solution.py
+++ b/solution.py
@@ -14,7 +14,7 @@
 SLICE = E // NY
 STEPS = 16
 SLOTS = 9
-NCH = 2
+NCH = 8
 CH = ROWS // NCH
 PAIRS = 16384.0
 
@@ -96,7 +96,6 @@
     pl.semaphore_wait(bar, len(peers))
 
     mine = 2 * y + h
-    send(x.at[1 - r], xg.at[mine], xg_ss.at[0], xg_rs.at[mine], at(xl, z, y, r, 1 - r))
     for d in range(1, NY):
         send(x.at[r], xg.at[mine], xg_ss.at[d], xg_rs.at[mine], at(xl, z, (y + d) % NY, r, r))
     send(x.at[r], xg.at[mine], xg_ss.at[4], xg_rs.at[mine], sibling, hh == 1)
@@ -107,10 +106,11 @@
 
     for copy in loads[2:]:
         copy.wait()
-    for k, tower in ((0, r), (1, 1 - r)):
+
+    def project(k, tower):
         features = x[tower]
 
-        def column(i, c, k=k, tower=tower, features=features):
+        def column(i, c):
             cols = pl.ds(pl.multiple_of(i * 256, 256), 256)
             p = jnp.dot(features, w[tower, :, cols], preferred_element_type=F32)
             part[k, :, cols] = p
@@ -118,22 +118,19 @@
             return c
 
         lax.fori_loop(0, E // 256, column, 0)
-        for c in range(NCH):
-            rows = pl.ds(c * CH, CH)
-            send(px_send.at[k, rows], px_recv.at[k, rows], px_ss.at[k, c], px_rs.at[k, c], partner)
-
-    for c in range(2):
-        slot = 2 * y + c
-
-        @pl.when(hh == 1)
-        def _():
-            arrived(xg.at[slot], xg_rs.at[slot])
-
-        for d in range(1, NY):
-            send(
-                xg.at[slot], xg.at[slot], xg_ss.at[4 + 3 * c + d], xg_rs.at[slot],
-                at(xl, z, (y + d) % NY, h, r), hh == 1,
-            )
+
+    def send_part(k, c):
+        rows = pl.ds(c * CH, CH)
+        send(px_send.at[k, rows], px_recv.at[k, rows], px_ss.at[k, c], px_rs.at[k, c], partner)
+
+    project(0, r)
+    PX0 = len(pending)
+    for c in range(3):
+        send_part(0, c)
+    project(1, 1 - r)
+    for c in range(3, NCH):
+        pending.pop(PX0)()
+        send_part(0, c)
 
     def slot_rows(j, c):
         return pl.ds(pl.multiple_of(j * ROWS + c * CH, CH), CH)
@@ -142,27 +139,47 @@
         return mirrored(plane * 8 + ((my + d) % NY) * 2 + hh)
 
     z_peer = mirrored((m + 120) % 128)
+
+    def pass_z(j, k, c, when=None):
+        src = buf.at[slot_rows(j, c)]
+        send(src, buf.at[slot_rows(j + 4, c)], zs_ss.at[k, c], bf_rs.at[j + 4, c], z_peer, when)
+
+    def pass_y(j, d, k, c, slot, when=None):
+        src = buf.at[slot_rows(j, c)]
+        send(src, buf.at[slot_rows(slot, c)], ys_ss.at[k, d - 1, c], bf_rs.at[slot, c], y_peer(d), when)
+
+    def block(j, c):
+        arrived(buf.at[slot_rows(j, c)], bf_rs.at[j, c])
+
+    last_plane = plane % NZ == NZ - 1
 
     for c in range(NCH):
         rows = pl.ds(c * CH, CH)
         arrived(px_recv.at[0, rows], px_rs.at[0, c])
+        if c == NCH - 1:
+            for k in range(NCH):
+                send_part(1, k)
         yy = part[1, rows, :] + px_recv[0, rows, :].astype(F32)
         inv = lax.rsqrt(jnp.sum(yy * yy, axis=-1, keepdims=True) + 1e-06)
         buf[slot_rows(0, c), :] = (yy * inv).astype(BF16)
-        src = buf.at[slot_rows(0, c)]
-        send(src, buf.at[slot_rows(4, c)], zs_ss.at[0, c], bf_rs.at[4, c], z_peer)
-        for d in range(1, NY):
-            send(
-                src, buf.at[slot_rows(4 - d, c)], ys_ss.at[0, d - 1, c], bf_rs.at[4 - d, c],
-                y_peer(d), my + d >= NY,
-            )
+        pass_z(0, 0, c)
+        for d in (2, 1, 3):
+            pass_y(0, d, 0, c, 4 - d, my + d >= NY)
     for c in range(NCH):
-        src = buf.at[slot_rows(4, c)]
-        arrived(src, bf_rs.at[4, c])
-        send(src, buf.at[slot_rows(8, c)], zs_ss.at[1, c], bf_rs.at[8, c], z_peer)
-        for d in range(1, NY):
-            slot = 4 - d + 4 * ((my + d) // NY)
-            send(src, buf.at[slot_rows(slot, c)], ys_ss.at[1, d - 1, c], bf_rs.at[slot, c], y_peer(d))
+        block(4, c)
+        pass_z(4, 1, c)
+        pass_y(4, 2, 1, c, 2 + 4 * ((my + 2) // NY), jnp.logical_or(my + 2 < NY, last_plane))
+        for d in (1, 3):
+            pass_y(4, d, 1, c, 4 - d + 4 * ((my + d) // NY))
+    for c in range(NCH):
+        block(2, c)
+        pass_z(2, 2, c, plane % NZ != 0)
+    for c in range(NCH):
+        block(8, c)
+        for d in (1, 3):
+            pass_y(8, d, 2, c, 8 - d, my + d < NY)
+        pass_y(8, 2, 2, c, 6, jnp.logical_and(my + 2 < NY, last_plane))
+    send(x.at[1 - r], xg.at[mine], xg_ss.at[0], xg_rs.at[mine], at(xl, z, y, r, 1 - r))
     for c in range(NCH):
         rows = pl.ds(c * CH, CH)
         arrived(px_recv.at[1, rows], px_rs.at[1, c])
@@ -173,21 +190,13 @@
         inv_own[rows, :] = inv
         own[hh, rows, :] = unit.astype(BF16)
     send(own.at[hh], own.at[hh], ow_ss, ow_rs, sibling)
-    for c in range(NCH):
-        src = buf.at[slot_rows(8, c)]
-        arrived(src, bf_rs.at[8, c])
-        for d in range(1, NY):
-            send(
-                src, buf.at[slot_rows(8 - d, c)], ys_ss.at[2, d - 1, c], bf_rs.at[8 - d, c],
-                y_peer(d), my + d < NY,
-            )
     arrived(own.at[1 - hh], ow_rs)
 
     scale, bias = scale_ref[0, 0], bias_ref[0, 0]
-    for j in (0, 4, 8, 3, 2, 1, 7, 6, 5):
-        if j not in (0, 4, 8):
+    for j in (0, 4, 8, 2, 3, 1, 7, 5, 6):
+        if j not in (0, 4, 8, 2):
             for c in range(NCH):
-                arrived(buf.at[slot_rows(j, c)], bf_rs.at[j, c])
+                block(j, c)
         cols = pl.ds(j * ROWS, ROWS)
         for a in range(2):
             dots = contract(own[a], buf[cols, :], 1, 1)
@@ -204,6 +213,19 @@
             offset = 2 * j + hh - a
             met = jnp.logical_and(offset >= 0, offset < STEPS)
             weights[a, :, cols] = jnp.where(met, scale * grad, 0.0).astype(BF16)
+
+    for c in range(2):
+        slot = 2 * y + c
+
+        @pl.when(hh == 1)
+        def _():
+            arrived(xg.at[slot], xg_rs.at[slot])
+
+        for d in range(1, NY):
+            send(
+                xg.at[slot], xg.at[slot], xg_ss.at[4 + 3 * c + d], xg_rs.at[slot],
+                at(xl, z, (y + d) % NY, h, r), hh == 1,
+            )
 
     for k, a in ((0, 1 - hh), (1, hh)):
         weighted = weights[a]
@@ -312,12 +334,17 @@
         finish()
 
 
+def hand_over(*refs):
+    for i in range(4):
+        refs[4 + i][...] = refs[i][...]
+
+
 def local(image_in, text_in, image_w, text_w, logit_scale, logit_bias):
-    hbm = pl.BlockSpec(memory_space=pl.ANY)
+    hbm = pl.BlockSpec(memory_space=pltpu.HBM)
     vmem = pl.BlockSpec(memory_space=pltpu.VMEM)
     smem = pl.BlockSpec(memory_space=pltpu.SMEM)
     dma = pltpu.SemaphoreType.DMA
-    return pl.pallas_call(
+    results = pl.pallas_call(
         body,
         name="contrast",
         out_shape=(
@@ -358,7 +385,7 @@
             dma((8,)),
             dma((2, NCH)),
             dma((2, NCH)),
-            dma((2, NCH)),
+            dma((3, NCH)),
             dma((3, 3, NCH)),
             dma((SLOTS, NCH)),
             dma, dma,
@@ -374,9 +401,16 @@
             dma((2, NY)),
         ],
         compiler_params=pltpu.CompilerParams(
-            collective_id=0, has_side_effects=True, vmem_limit_bytes=48 << 20
+            collective_id=0, has_side_effects=True, vmem_limit_bytes=60 << 20
         ),
     )(image_in, text_in, image_w, text_w, logit_scale.reshape(1, 1), logit_bias.reshape(1, 1))
+    return pl.pallas_call(
+        hand_over,
+        name="hand_over",
+        out_shape=tuple(jax.ShapeDtypeStruct(q.shape, q.dtype) for q in results),
+        in_specs=[vmem] * 4,
+        out_specs=(vmem,) * 4,
+    )(*results)
 
 
 def solution(mesh):

time: 110 us -> 97.6 us (0.89)
  local copies, waits for them, and re-layouts: 7.77 us -> 0 us
  Pallas kernels: 100 us -> 95.6 us
    unnamed x12 -> x0, local copies, waits for them, and re-layouts: 7.77 us -> none
    pallas_call x1, Pallas kernels: 100 us -> 93.8 us  [local(): pl.pallas_call(body, name='contrast', out_shape=(jax.ShapeDtypeStruct((RO...]
    pallas_call x0 -> x1, Pallas kernels: none -> 1.81 us  [local(): pl.pallas_call(hand_over, name='hand_over', out_shape=tuple((jax.ShapeDty...]
where the time goes in v2:
time: 97.6 us; the launch traced here: 97.5 us
  Pallas kernels  95.6 us (98%)
  between operations  1.93 us (2%)
    pallas_call x1, Pallas kernels, local(): pl.pallas_call(body, name='contrast', out_shape=(jax.ShapeDtypeStruct((RO...  93.8 us

profile of v2, /device:TPU:1, one launch (start us, length us, event | category | flops | bytes accessed | tf_op | source)
XLA Modules:
  0.0 97.5 jit_solution(6142897170497165352)
XLA Ops:
  1.9 93.8 %contrast.1 = (bf16[128,768]{1,0:T(8,128)(2,1)}, bf16[128,768]{1,0:T(8,128)(2,1)}, f32[6,1536]{1,0:T(8,128)}, f32[6,1536]{1,0:T(8,128)}) custom-call(bf16[128,768]{1,0:T(8,128)(2,1)} %image_in.1, bf16[128,768]{1,0:T(8,128)(2,1)} %text_in.1, bf16[768,1536]{1,0:T(8,128)(2,1)} %image_w.1, bf16[768,1536]{1,0:T(8,128)(2,1)} %text_w.1, f32[1,1]{1,0:T(1,128)} %bitcast.2.scale_ref, ...), custom_call_target="tpu_custom_call" | custom-call | tf_op jit(solution)/shard_map/contrast/pallas_call | solution.py:347
  95.7 1.8 %hand_over.1 = (bf16[128,768]{1,0:T(8,128)(2,1)}, bf16[128,768]{1,0:T(8,128)(2,1)}, f32[6,1536]{1,0:T(8,128)}, f32[6,1536]{1,0:T(8,128)}) custom-call(bf16[128,768]{1,0:T(8,128)(2,1)} %get-tuple-element.8.refs_0_, bf16[128,768]{1,0:T(8,128)(2,1)} %get-tuple-element.9.refs_1_, f32[6,1536]{1,0:T(8,128)} %get-tuple-element.10.refs_2_, ...), custom_call_target="tpu_custom_call" | custom-call | tf_op jit(solution)/shard_map/hand_over/pallas_call | solution.py:407

commit v3 on v2

--- a/solution.py
+++ b/solution.py
@@ -168,17 +168,18 @@
     for c in range(NCH):
         block(4, c)
         pass_z(4, 1, c)
-        pass_y(4, 2, 1, c, 2 + 4 * ((my + 2) // NY), jnp.logical_or(my + 2 < NY, last_plane))
+        pass_y(4, 2, 1, c, 2 + 4 * ((my + 2) // NY), jnp.logical_or(my + 2 < NY, last_plane) if c % 2 == 1 else my + 2 < NY)
         for d in (1, 3):
             pass_y(4, d, 1, c, 4 - d + 4 * ((my + d) // NY))
     for c in range(NCH):
         block(2, c)
-        pass_z(2, 2, c, plane % NZ != 0)
+        pass_z(2, 2, c, (plane % NZ != 0) if c % 2 == 1 else None)
     for c in range(NCH):
         block(8, c)
         for d in (1, 3):
             pass_y(8, d, 2, c, 8 - d, my + d < NY)
-        pass_y(8, 2, 2, c, 6, jnp.logical_and(my + 2 < NY, last_plane))
+        if c % 2 == 1:
+            pass_y(8, 2, 2, c, 6, jnp.logical_and(my + 2 < NY, last_plane))
     send(x.at[1 - r], xg.at[mine], xg_ss.at[0], xg_rs.at[mine], at(xl, z, y, r, 1 - r))
     for c in range(NCH):
         rows = pl.ds(c * CH, CH)

time: 97.6 us -> 96.9 us (level)
  Pallas kernels: 95.6 us -> 94 us
    pallas_call x1, Pallas kernels: 93.8 us -> 92.2 us  [local(): pl.pallas_call(body, name='contrast', out_shape=(jax.ShapeDtypeStruct((RO...]
where the time goes in v3:
time: 96.9 us; the launch traced here: 95.9 us
  Pallas kernels  94 us (97%)
  between operations  1.93 us (2%)
    pallas_call x1, Pallas kernels, local(): pl.pallas_call(body, name='contrast', out_shape=(jax.ShapeDtypeStruct((RO...  92.2 us

profile of v3, /device:TPU:1, one launch (start us, length us, event | category | flops | bytes accessed | tf_op | source)
XLA Modules:
  0.0 95.9 jit_solution(16734924890338591339)
XLA Ops:
  1.9 92.2 %contrast.1 = (bf16[128,768]{1,0:T(8,128)(2,1)}, bf16[128,768]{1,0:T(8,128)(2,1)}, f32[6,1536]{1,0:T(8,128)}, f32[6,1536]{1,0:T(8,128)}) custom-call(bf16[128,768]{1,0:T(8,128)(2,1)} %image_in.1, bf16[128,768]{1,0:T(8,128)(2,1)} %text_in.1, bf16[768,1536]{1,0:T(8,128)(2,1)} %image_w.1, bf16[768,1536]{1,0:T(8,128)(2,1)} %text_w.1, f32[1,1]{1,0:T(1,128)} %bitcast.2.scale_ref, ...), custom_call_target="tpu_custom_call" | custom-call | tf_op jit(solution)/shard_map/contrast/pallas_call | solution.py:348
  94.1 1.8 %hand_over.1 = (bf16[128,768]{1,0:T(8,128)(2,1)}, bf16[128,768]{1,0:T(8,128)(2,1)}, f32[6,1536]{1,0:T(8,128)}, f32[6,1536]{1,0:T(8,128)}) custom-call(bf16[128,768]{1,0:T(8,128)(2,1)} %get-tuple-element.8.refs_0_, bf16[128,768]{1,0:T(8,128)(2,1)} %get-tuple-element.9.refs_1_, f32[6,1536]{1,0:T(8,128)} %get-tuple-element.10.refs_2_, ...), custom_call_target="tpu_custom_call" | custom-call | tf_op jit(solution)/shard_map/hand_over/pallas_call | solution.py:408
